TPU v7x, 32 devices: a whole 2x2x4 slice. The times are simulated.
32 devices in a mesh: lon: 8 (over y, x, core), lat: 4 (over z).
Axes of the slice: x: 2, y: 2, z: 4, core: 2. Of those that a mesh axis runs over, the one named last changes fastest.
Arguments:
- members: bfloat16 [80, 2, 128, 1024], P(None, None, 'lat', 'lon'), may hold values from -18 to 18
- gradient: float32 [2, 128, 1024], P(None, 'lat', 'lon'), may hold values from -6 to 6
- lon_taper: bfloat16 [513], replicated, as said below
- lat_taper: bfloat16 [129], replicated, as said below
Outputs:
- covariance_product: float32 [2, 128, 1024], P(None, 'lat', 'lon')
Inputs may be any that keep to these rules, and one draw needn't show every extreme that they name: lon_taper holds the weights of offsets -256 to 256 in that order; none is negative. lat_taper holds the weights of offsets -64 to 64 in that order; none is negative.
All inputs are finite; a program needn't handle non-finite values.
Results may differ from a plain program's by a relative error of at most 0.0041.
Values may be sent and summed in bfloat16 or wider, within the bound.
A program may use at most 64 MiB of HBM per device.

v0:
```python
import jax
import jax.numpy as jnp
from jax import lax
from jax.sharding import PartitionSpec as P


def from_behind(value, axis, steps):
    count = lax.axis_size(axis)
    pairs = [(source, (source + steps) % count) for source in range(count)]
    return lax.ppermute(value, axis, pairs)


def from_behind_2(block, axis, distance):
    devices = range(lax.axis_size(axis))
    route = [(i - distance, i) for i in devices if i - distance in devices]
    return lax.ppermute(block, axis, route)


def taper_table(weights, block_cells):
    half = 2 * block_cells
    rows_at = jnp.arange(5 * block_cells, dtype=jnp.int32)[:, None]
    cols_at = jnp.arange(block_cells, dtype=jnp.int32)[None, :]
    dist = cols_at + half - rows_at
    where_at = jnp.clip(dist + half, 0, 2 * half)
    picked = jnp.take(weights, where_at, axis=0)
    return jnp.where(jnp.abs(dist) <= half, picked, jnp.zeros_like(picked))


def cycle_blocks(values):
    pieces = {}
    for offset in (2, 1, -1, -2):
        pieces[offset] = from_behind(values, "lon", offset)
    return jnp.concatenate([pieces[2], pieces[1], values, pieces[-1], pieces[-2]], axis=3)


def line_blocks(values):
    pieces = {}
    for offset in (2, 1, -1, -2):
        pieces[offset] = from_behind_2(values, "lat", offset)
    return jnp.concatenate([pieces[2], pieces[1], values, pieces[-1], pieces[-2]], axis=2)


def per_device(members, gradient, lon_taper, lat_taper):
    clat = gradient.shape[1]
    clon = gradient.shape[2]
    count = members.shape[0]
    products = (members.astype(jnp.float32) * gradient).astype(jnp.bfloat16)
    lon_table = taper_table(lon_taper, clon)
    extended = cycle_blocks(products)
    along_lon = jnp.einsum(
        "mlae,ei->mlai", extended, lon_table, preferred_element_type=jnp.float32
    ).astype(jnp.bfloat16)
    lat_table = taper_table(lat_taper, clat)
    rimmed = line_blocks(along_lon)
    along_lat = jnp.einsum("mlec,ea->mlac", rimmed, lat_table, preferred_element_type=jnp.float32)
    weighted = jnp.sum(members.astype(jnp.float32) * along_lat, axis=0)
    return weighted / (count - 1)


def solution(mesh):
    in_specs = (P(None, None, "lat", "lon"), P(None, "lat", "lon"), P(), P())
    out_specs = P(None, "lat", "lon")
    return jax.shard_map(
        per_device, mesh=mesh, in_specs=in_specs, out_specs=out_specs, check_vma=False
    )
```

profile of v0, /device:TPU:0, one launch (start us, length us, event | category | flops | bytes accessed | tf_op | source)
XLA Modules:
  0.0 619.8 jit_solution(6561874816807331146)
XLA Ops:
  0.0 0.0 copy-start
  0.0 2.8 fusion
  2.8 2.9 collective-permute-start
  5.7 0.0 collective-permute-start.1
  5.7 2.6 collective-permute-start.2
  8.4 0.1 collective-permute-start.3
  8.5 0.2 fusion.3
  8.6 0.0 copy-done
  8.7 0.0 copy-start.2
  8.7 0.0 copy-start.3
  8.7 502.4 %gather_fusion.1 = bf16[81920]{0:T(1024)(128)(2,1)S(1)} fusion(bf16[513]{0:T(1024)(128)(2,1)S(1)} %copy-done, s32[81920]{0:T(1024)S(1)} %fusion.3), kind=kCustom, calls=%fused_computation.1 | custom fusion | bytes 655360 | tf_op jit(solution)/shard_map/jit(_take)/gather | solution.py:25
  511.1 0.0 collective-permute-done
  511.1 1.6 constant_dynamic-update-slice_fusion.4
  512.7 0.0 collective-permute-done.1
  512.7 1.8 constant_dynamic-update-slice_fusion.3
  514.5 0.0 copy-done.2
  514.5 0.0 copy-done.3
  514.5 0.6 constant_dynamic-update-slice_fusion.2
  515.1 0.0 collective-permute-done.2
  515.1 1.8 constant_dynamic-update-slice_fusion.1
  516.8 0.0 collective-permute-done.3
  516.9 0.5 constant_dynamic-update-slice_fusion
  517.3 0.0 copy-start.1
  517.3 1.9 convolution_convert_fusion
  519.3 6.0 collective-permute-start.4
  525.3 4.5 collective-permute-start.5
  529.8 1.3 collective-permute-start.6
  531.1 1.3 collective-permute-start.7
  532.5 0.1 reshape.133
  532.6 0.0 copy-done.1
  532.6 30.4 %gather_fusion = bf16[5120]{0:T(1024)(128)(2,1)S(1)} fusion(bf16[129]{0:T(256)(128)(2,1)S(1)} %copy-done.1, s32[5120]{0:T(1024)S(1)} %broadcast_clamp_fusion), kind=kCustom, calls=%fused_computation | custom fusion | bytes 40960 | tf_op jit(solution)/shard_map/jit(_take)/gather | solution.py:25
  563.0 0.1 reshape.132
  563.1 0.0 collective-permute-done.4
  563.1 1.6 constant_dynamic-update-slice_fusion.9
  564.6 15.5 %collective-permute-done.5 = bf16[80,2,32,128]{3,2,1,0:T(8,128)(2,1)} collective-permute-done((bf16[80,2,32,128]{3,2,1,0:T(8,128)(2,1)S(1)}, bf16[80,2,32,128]{3,2,1,0:T(8,128)(2,1)}, u32[]{:S(2)}, u32[]{:S(2)}) %collective-permute-start.5) | collective-permute-done | bytes 1310752 | tf_op jit(solution)/shard_map/ppermute | solution.py:16
  580.2 1.6 constant_dynamic-update-slice_fusion.8
  581.8 0.3 constant_dynamic-update-slice_fusion.7
  582.1 0.0 collective-permute-done.6
  582.1 1.6 constant_dynamic-update-slice_fusion.6
  583.8 32.7 %collective-permute-done.7 = bf16[80,2,32,128]{3,2,1,0:T(8,128)(2,1)} collective-permute-done((bf16[80,2,32,128]{3,2,1,0:T(8,128)(2,1)S(1)}, bf16[80,2,32,128]{3,2,1,0:T(8,128)(2,1)}, u32[]{:S(2)}, u32[]{:S(2)}) %collective-permute-start.7) | collective-permute-done | bytes 1310752 | tf_op jit(solution)/shard_map/ppermute | solution.py:16
  616.4 1.6 constant_dynamic-update-slice_fusion.5
  618.1 1.1 fusion.1
  619.2 0.6 broadcast_multiply_fusion
  (4 shorter events, 0.0 us)
Async XLA Ops:
  0.0 8.6 %copy-start = (bf16[513]{0:T(1024)(128)(2,1)S(1)}, bf16[513]{0:T(1024)(128)(2,1)}, u32[]{:S(2)}) copy-start(bf16[513]{0:T(1024)(128)(2,1)} %param.6) | copy-start | bytes 3082
  2.8 508.3 %collective-permute-start = (bf16[80,2,32,128]{3,2,1,0:T(8,128)(2,1)}, bf16[80,2,32,128]{3,2,1,0:T(8,128)(2,1)}, u32[]{:S(2)}, u32[]{:S(2)}) collective-permute-start(bf16[80,2,32,128]{3,2,1,0:T(8,128)(2,1)} %fusion), channel_id=1, source_target_pairs={{0,8},{4,12},{8,16},{12,20},{16,24},{20,28},{24,0},{28,4},{1,9},{5... | collective-permute-start | bytes 3932168 | tf_op jit(solution)/shard_map/ppermute | solution.py:10
  5.7 506.9 %collective-permute-start.1 = (bf16[80,2,32,128]{3,2,1,0:T(8,128)(2,1)}, bf16[80,2,32,128]{3,2,1,0:T(8,128)(2,1)}, u32[]{:S(2)}, u32[]{:S(2)}) collective-permute-start(bf16[80,2,32,128]{3,2,1,0:T(8,128)(2,1)} %fusion), channel_id=1, source_target_pairs={{0,4},{4,8},{8,12},{12,16},{16,20},{20,24},{24,28},{28,0},{1,5},{5... | collective-permute-start | bytes 3932168 | tf_op jit(solution)/shard_map/ppermute | solution.py:10
  5.7 509.3 %collective-permute-start.2 = (bf16[80,2,32,128]{3,2,1,0:T(8,128)(2,1)}, bf16[80,2,32,128]{3,2,1,0:T(8,128)(2,1)}, u32[]{:S(2)}, u32[]{:S(2)}) collective-permute-start(bf16[80,2,32,128]{3,2,1,0:T(8,128)(2,1)} %fusion), channel_id=1, source_target_pairs={{0,28},{4,0},{8,4},{12,8},{16,12},{20,16},{24,20},{28,24},{1,29},{... | collective-permute-start | bytes 3932168 | tf_op jit(solution)/shard_map/ppermute | solution.py:10
  8.4 508.5 %collective-permute-start.3 = (bf16[80,2,32,128]{3,2,1,0:T(8,128)(2,1)}, bf16[80,2,32,128]{3,2,1,0:T(8,128)(2,1)S(1)}, u32[]{:S(2)}, u32[]{:S(2)}) collective-permute-start(bf16[80,2,32,128]{3,2,1,0:T(8,128)(2,1)} %fusion), channel_id=1, source_target_pairs={{0,24},{4,28},{8,0},{12,4},{16,8},{20,12},{24,16},{28,20},{1,25},{... | collective-permute-start | bytes 3932168 | tf_op jit(solution)/shard_map/ppermute | solution.py:10
  8.7 505.8 %copy-start.2 = (bf16[80,2,32,128]{3,2,1,0:T(8,128)(2,1)S(1)}, bf16[80,2,32,128]{3,2,1,0:T(8,128)(2,1)}, u32[]{:S(2)}) copy-start(bf16[80,2,32,128]{3,2,1,0:T(8,128)(2,1)} %param.4) | copy-start | bytes 3932164
  8.7 505.8 %copy-start.3 = (f32[2,32,128]{2,1,0:T(8,128)S(1)}, f32[2,32,128]{2,1,0:T(8,128)}, u32[]{:S(2)}) copy-start(f32[2,32,128]{2,1,0:T(8,128)} %param.5) | copy-start | bytes 98308
  517.3 15.3 %copy-start.1 = (bf16[129]{0:T(256)(128)(2,1)S(1)}, bf16[129]{0:T(256)(128)(2,1)}, u32[]{:S(2)}) copy-start(bf16[129]{0:T(256)(128)(2,1)} %param.7) | copy-start | bytes 778
  519.3 43.8 %collective-permute-start.4 = (bf16[80,2,32,128]{3,2,1,0:T(8,128)(2,1)S(1)}, bf16[80,2,32,128]{3,2,1,0:T(8,128)(2,1)}, u32[]{:S(2)}, u32[]{:S(2)}) collective-permute-start(bf16[80,2,32,128]{3,2,1,0:T(8,128)(2,1)S(1)} %convolution_convert_fusion), channel_id=1, source_target_pairs={{0,2},{1,3},{4,6},{5,7},{8,10},{9,11},{12,14},{13,15},{16,18},{17,... | collective-permute-start | bytes 3932168 | tf_op jit(solution)/shard_map/ppermute | solution.py:16
  525.3 54.8 %collective-permute-start.5 = (bf16[80,2,32,128]{3,2,1,0:T(8,128)(2,1)S(1)}, bf16[80,2,32,128]{3,2,1,0:T(8,128)(2,1)}, u32[]{:S(2)}, u32[]{:S(2)}) collective-permute-start(bf16[80,2,32,128]{3,2,1,0:T(8,128)(2,1)S(1)} %convolution_convert_fusion), channel_id=1, source_target_pairs={{0,1},{1,2},{2,3},{4,5},{5,6},{6,7},{8,9},{9,10},{10,11},{12,13},{... | collective-permute-start | bytes 3932168 | tf_op jit(solution)/shard_map/ppermute | solution.py:16
  529.8 52.3 %collective-permute-start.6 = (bf16[80,2,32,128]{3,2,1,0:T(8,128)(2,1)S(1)}, bf16[80,2,32,128]{3,2,1,0:T(8,128)(2,1)}, u32[]{:S(2)}, u32[]{:S(2)}) collective-permute-start(bf16[80,2,32,128]{3,2,1,0:T(8,128)(2,1)S(1)} %convolution_convert_fusion), channel_id=1, source_target_pairs={{1,0},{2,1},{3,2},{5,4},{6,5},{7,6},{9,8},{10,9},{11,10},{13,12},{... | collective-permute-start | bytes 3932168 | tf_op jit(solution)/shard_map/ppermute | solution.py:16
  531.1 85.3 %collective-permute-start.7 = (bf16[80,2,32,128]{3,2,1,0:T(8,128)(2,1)S(1)}, bf16[80,2,32,128]{3,2,1,0:T(8,128)(2,1)}, u32[]{:S(2)}, u32[]{:S(2)}) collective-permute-start(bf16[80,2,32,128]{3,2,1,0:T(8,128)(2,1)S(1)} %convolution_convert_fusion), channel_id=1, source_target_pairs={{2,0},{3,1},{6,4},{7,5},{10,8},{11,9},{14,12},{15,13},{18,16},{19,... | collective-permute-start | bytes 3932168 | tf_op jit(solution)/shard_map/ppermute | solution.py:16
where the time goes:
time: 620 us
  local copies, waits for them, and re-layouts  545 us (88%)
  waiting for transfers between devices  48.2 us (8%)
  starting transfers between devices  18.8 us (3%)
    gather x3, local copies, waits for them, and re-layouts, taper_table(): picked = jnp.take(weights, where_at, axis=0)  533 us
    ppermute x4, waiting for transfers between devices, from_behind_2(): return lax.ppermute(block, axis, route)  48.2 us
    ppermute x4, starting transfers between devices, from_behind_2(): return lax.ppermute(block, axis, route)  13.1 us
  transfers between devices with their start and end apart: 8, of which 2 were waited for; matrix products, arithmetic and copies ran while one was open for 88% of the time, Pallas kernels for 0%

commit v1 on v0

--- a/solution.py
+++ b/solution.py
@@ -1,7 +1,13 @@
+import functools
+
 import jax
 import jax.numpy as jnp
 from jax import lax
+from jax.experimental import pallas as pl
+from jax.experimental.pallas import tpu as pltpu
 from jax.sharding import PartitionSpec as P
+
+MESH = pl.DeviceIdType.MESH
 
 
 def from_behind(value, axis, steps):
@@ -40,7 +46,7 @@
     return jnp.concatenate([pieces[2], pieces[1], values, pieces[-1], pieces[-2]], axis=2)
 
 
-def per_device(members, gradient, lon_taper, lat_taper):
+def halo_plan(members, gradient, lon_taper, lat_taper):
     clat = gradient.shape[1]
     clon = gradient.shape[2]
     count = members.shape[0]
@@ -57,6 +63,223 @@
     return weighted / (count - 1)
 
 
+def member_kernel(
+    n_lon, n_lat, count,
+    members, gradient, lon_line, lat_line, out,
+    grad_z, grad_all, taken, wide, lon_table, lat_table, partial, parts,
+    gz_send, gz_recv, ga_send, ga_recv, m_send, m_recv, r_send, r_recv, own_sem,
+):
+    i, j = lax.axis_index("lon"), lax.axis_index("lat")
+    clat, clon = gradient.shape[1], gradient.shape[2]
+    n = n_lon * n_lat
+    share = taken.shape[1]
+    lat_cells = n_lat * clat
+    me = i * n_lat + j
+    level = lax.rem(i, 2)
+
+    def shares_of(i_to, j_to):
+        return ((i_to // 2) * n_lat + j_to) * share
+
+    def other(k):
+        i_to = lax.rem(i + k // n_lat, n_lon)
+        j_to = lax.rem(j + lax.rem(k, n_lat), n_lat)
+        return i_to, j_to
+
+    barrier = pltpu.get_barrier_semaphore()
+
+    def greet(k, c):
+        i_to, j_to = other(k)
+        pl.semaphore_signal(barrier, inc=1, device_id={"lon": i_to, "lat": j_to}, device_id_type=MESH)
+        return c
+
+    lax.fori_loop(1, n, greet, 0)
+    pl.semaphore_wait(barrier, n - 1)
+
+    def grad_z_copy(k):
+        j_to = lax.rem(j + k, n_lat)
+        return pltpu.make_async_remote_copy(
+            src_ref=gradient, dst_ref=grad_z.at[j],
+            send_sem=gz_send.at[j_to], recv_sem=gz_recv.at[j],
+            device_id={"lon": i, "lat": j_to}, device_id_type=MESH,
+        )
+
+    for k in range(1, n_lat):
+        grad_z_copy(k).start()
+
+    def member_copy(k):
+        i_to, j_to = other(k)
+        return pltpu.make_async_remote_copy(
+            src_ref=members.at[pl.ds(shares_of(i_to, j_to), share), lax.rem(i_to, 2)],
+            dst_ref=taken.at[i, :, pl.ds(pl.multiple_of(j * clat, clat), clat), :],
+            send_sem=m_send.at[i_to * n_lat + j_to], recv_sem=m_recv.at[me],
+            device_id={"lon": i_to, "lat": j_to}, device_id_type=MESH,
+        )
+
+    def start_members(k, c):
+        member_copy(k).start()
+        return c
+
+    lax.fori_loop(1, n, start_members, 0)
+    own = pltpu.make_async_copy(
+        members.at[pl.ds(shares_of(i, j), share), level],
+        taken.at[i, :, pl.ds(pl.multiple_of(j * clat, clat), clat), :],
+        own_sem,
+    )
+    own.start()
+    grad_z[j] = gradient[...]
+
+    for k in range(1, n_lat):
+        j_from = lax.rem(j + k, n_lat)
+        pltpu.make_async_remote_copy(
+            src_ref=gradient, dst_ref=grad_z.at[j_from],
+            send_sem=gz_send.at[j_from], recv_sem=gz_recv.at[j_from],
+            device_id={"lon": i, "lat": j_from}, device_id_type=MESH,
+        ).wait()
+
+    def grad_all_copy(k):
+        i_to = lax.rem(i + k, n_lon)
+        return pltpu.make_async_remote_copy(
+            src_ref=grad_z.at[:, lax.rem(i_to, 2)], dst_ref=grad_all.at[i],
+            send_sem=ga_send.at[i_to], recv_sem=ga_recv.at[i],
+            device_id={"lon": i_to, "lat": j}, device_id_type=MESH,
+        )
+
+    for k in range(1, n_lon):
+        grad_all_copy(k).start()
+    grad_all[i] = grad_z[:, level]
+
+    rows, cols = lon_table.shape
+    line = lon_line.shape[1]
+    spread = jnp.broadcast_to(lon_line[...], (rows, line))
+    turned = pltpu.roll(spread, line - 4 * clon - 2 * clon, 1, stride=1, stride_axis=0)
+    lon_table[...] = turned[:, :cols].astype(jnp.bfloat16)
+    spread = jnp.broadcast_to(lat_line[...], (lat_cells, lat_line.shape[1]))
+    turned = pltpu.roll(spread, lat_line.shape[1] - lat_cells, 1, stride=1, stride_axis=0)
+    lat_table[...] = turned[:, :lat_cells].astype(jnp.bfloat16)
+
+    for k in range(1, n_lon):
+        i_from = lax.rem(i + k, n_lon)
+        pltpu.make_async_remote_copy(
+            src_ref=grad_z.at[:, 0], dst_ref=grad_all.at[i_from],
+            send_sem=ga_send.at[i_from], recv_sem=ga_recv.at[i_from],
+            device_id={"lon": i_from, "lat": j}, device_id_type=MESH,
+        ).wait()
+
+    own.wait()
+
+    def wait_members(k, c):
+        i_from, j_from = other(k)
+        s = i_from * n_lat + j_from
+        pltpu.make_async_remote_copy(
+            src_ref=members.at[pl.ds(0, share), 0],
+            dst_ref=taken.at[i_from, :, pl.ds(pl.multiple_of(j_from * clat, clat), clat), :],
+            send_sem=m_send.at[s], recv_sem=m_recv.at[s],
+            device_id={"lon": i_from, "lat": j_from}, device_id_type=MESH,
+        ).wait()
+        return c
+
+    lax.fori_loop(1, n, wait_members, 0)
+
+    for b in range(n_lon):
+        g = grad_all[b].reshape(lat_cells, clon)
+        p = (taken[b].astype(jnp.float32) * g[None]).astype(jnp.bfloat16)
+        p = p.reshape(share * lat_cells, clon)
+        for at in (b - n_lon + 2, b + 2, b + n_lon + 2):
+            if 0 <= at < n_lon + 4:
+                wide[:, at * clon:(at + 1) * clon] = p
+
+    for o in range(n_lon // 2):
+        along_lon = jnp.dot(
+            wide[:, 2 * o * clon:(2 * o + 6) * clon], lon_table[...],
+            preferred_element_type=jnp.float32,
+        ).astype(jnp.bfloat16)
+        total = jnp.zeros((lat_cells, 2 * clon), jnp.float32)
+        for m in range(share):
+            along_lat = jnp.dot(
+                lat_table[...], along_lon[m * lat_cells:(m + 1) * lat_cells],
+                preferred_element_type=jnp.float32,
+            )
+            x = jnp.concatenate([taken[2 * o, m], taken[2 * o + 1, m]], axis=1)
+            total += x.astype(jnp.float32) * along_lat
+        partial[2 * o] = total[:, :clon].astype(jnp.bfloat16)
+        partial[2 * o + 1] = total[:, clon:].astype(jnp.bfloat16)
+
+    def part_copy(k):
+        i_to, j_to = other(k)
+        return pltpu.make_async_remote_copy(
+            src_ref=partial.at[i_to, pl.ds(pl.multiple_of(j_to * clat, clat), clat), :],
+            dst_ref=parts.at[level, (i // 2) * n_lat + j],
+            send_sem=r_send.at[i_to * n_lat + j_to], recv_sem=r_recv.at[me],
+            device_id={"lon": i_to, "lat": j_to}, device_id_type=MESH,
+        )
+
+    def start_parts(k, c):
+        part_copy(k).start()
+        return c
+
+    lax.fori_loop(1, n, start_parts, 0)
+    parts[level, (i // 2) * n_lat + j] = partial[i, pl.ds(pl.multiple_of(j * clat, clat), clat), :]
+
+    def wait_parts(k, c):
+        i_from, j_from = other(k)
+        s = i_from * n_lat + j_from
+        pltpu.make_async_remote_copy(
+            src_ref=partial.at[i_from, pl.ds(pl.multiple_of(j_from * clat, clat), clat), :],
+            dst_ref=parts.at[lax.rem(i_from, 2), (i_from // 2) * n_lat + j_from],
+            send_sem=r_send.at[s], recv_sem=r_recv.at[s],
+            device_id={"lon": i_from, "lat": j_from}, device_id_type=MESH,
+        ).wait()
+        return c
+
+    lax.fori_loop(1, n, wait_parts, 0)
+    for l in range(2):
+        out[l] = jnp.sum(parts[l].astype(jnp.float32), axis=0) / (count - 1)
+
+
+def member_plan(members, gradient, lon_taper, lat_taper):
+    n_lon, n_lat = lax.axis_size("lon"), lax.axis_size("lat")
+    count, levels, clat, clon = members.shape
+    share = count // (n_lon // 2 * n_lat)
+    lat_cells = n_lat * clat
+    line = 8 * clon
+    lon_line = jnp.pad(lon_taper.astype(jnp.float32), (2 * clon, line - 6 * clon - 1))[None]
+    side = lat_cells - 2 * clat
+    lat_line = jnp.pad(lat_taper[::-1].astype(jnp.float32), (side, side - 1))[None]
+    n = n_lon * n_lat
+    vmem = pl.BlockSpec(memory_space=pltpu.VMEM)
+    dma = pltpu.SemaphoreType.DMA
+    return pl.pallas_call(
+        functools.partial(member_kernel, n_lon, n_lat, count),
+        out_shape=jax.ShapeDtypeStruct(gradient.shape, jnp.float32),
+        in_specs=[pl.BlockSpec(memory_space=pl.ANY), vmem, vmem, vmem],
+        out_specs=vmem,
+        scratch_shapes=[
+            pltpu.VMEM((n_lat, levels, clat, clon), jnp.float32),
+            pltpu.VMEM((n_lon, n_lat, clat, clon), jnp.float32),
+            pltpu.VMEM((n_lon, share, lat_cells, clon), jnp.bfloat16),
+            pltpu.VMEM((share * lat_cells, (n_lon + 4) * clon), jnp.bfloat16),
+            pltpu.VMEM((6 * clon, 2 * clon), jnp.bfloat16),
+            pltpu.VMEM((lat_cells, lat_cells), jnp.bfloat16),
+            pltpu.VMEM((n_lon, lat_cells, clon), jnp.bfloat16),
+            pltpu.VMEM((2, n // 2, clat, clon), jnp.bfloat16),
+            dma((n_lat,)), dma((n_lat,)), dma((n_lon,)), dma((n_lon,)),
+            dma((n,)), dma((n,)), dma((n,)), dma((n,)), dma,
+        ],
+        compiler_params=pltpu.CompilerParams(
+            collective_id=0, has_side_effects=True, vmem_limit_bytes=40 * 1024 * 1024
+        ),
+    )(members, gradient, lon_line, lat_line)
+
+
+def per_device(members, gradient, lon_taper, lat_taper):
+    n_lon, n_lat = lax.axis_size("lon"), lax.axis_size("lat")
+    count, levels, clat, clon = members.shape
+    even = levels == 2 and n_lon % 2 == 0 and n_lon >= 6
+    if even and count % (n_lon // 2 * n_lat) == 0 and n_lat * clat % 128 == 0 and n_lat >= 3:
+        return member_plan(members, gradient, lon_taper, lat_taper)
+    return halo_plan(members, gradient, lon_taper, lat_taper)
+
+
 def solution(mesh):
     in_specs = (P(None, None, "lat", "lon"), P(None, "lat", "lon"), P(), P())
     out_specs = P(None, "lat", "lon")

time: 620 us -> 55.7 us (0.09)
  local copies, waits for them, and re-layouts: 545 us -> 3.51 us
  Pallas kernels: 0 us -> 51.2 us
  waiting for transfers between devices: 48.2 us -> 0 us
  starting transfers between devices: 18.8 us -> 0 us
    gather x3 -> x0, local copies, waits for them, and re-layouts: 533 us -> none  [taper_table(): picked = jnp.take(weights, where_at, axis=0)]
    pallas_call x0 -> x1, Pallas kernels: none -> 51.2 us  [member_plan(): pl.pallas_call(functools.partial(member_kernel, n_lon, n_lat, count), out...]
    ppermute x8 -> x0, waiting for transfers between devices: 48.2 us -> none  [the longest x4 48.2 us: from_behind_2(): return lax.ppermute(block, axis, route)]
    ppermute x8 -> x0, starting transfers between devices: 18.8 us -> none  [the longest x4 13.1 us: from_behind_2(): return lax.ppermute(block, axis, route)]
    unnamed x15 -> x7, local copies, waits for them, and re-layouts: 10.3 us -> 3.51 us
  transfers between devices with their start and end apart: 8 -> 0, of which waited for: 2 -> 0; matrix products, arithmetic and copies ran while one was open for 88% -> 0% of each run, Pallas kernels for 0% -> 0%
where the time goes in v1:
time: 55.7 us; the launch traced here: 55.5 us
  Pallas kernels  51.2 us (92%)
  local copies, waits for them, and re-layouts  3.51 us (6%)
  other arithmetic  0.76 us (1%)
    pallas_call x1, Pallas kernels, member_plan(): pl.pallas_call(functools.partial(member_kernel, n_lon, n_lat, count), out...  51.2 us
    unnamed x7, local copies, waits for them, and re-layouts  3.51 us

profile of v1, /device:TPU:0, one launch (start us, length us, event | category | flops | bytes accessed | tf_op | source)
XLA Modules:
  0.0 55.5 jit_solution(12521041295129376631)
XLA Ops:
  0.0 0.7 %reverse = bf16[256]{0:T(256)(128)(2,1)S(1)} reverse(bf16[256]{0:T(256)(128)(2,1)} %bitcast.5), dimensions={0} | reverse | bytes 1024
  0.7 0.1 slice
  0.8 0.1 pad_convert_fusion.1
  0.9 0.7 %pad_convert_fusion = f32[1024]{0:T(1024)S(1)} fusion(bf16[513]{0:T(1024)(128)(2,1)} %param.6), kind=kLoop, calls=%fused_computation | loop fusion | flops 1024 | bytes 5122 | tf_op jit(solution)/shard_map/broadcast_in_dim | solution.py:245
  1.6 0.0 copy-start
  1.6 1.3 %copy-done = bf16[80,2,32,128]{3,2,1,0:T(8,128)(2,1)S(1)} copy-done((bf16[80,2,32,128]{3,2,1,0:T(8,128)(2,1)S(1)}, bf16[80,2,32,128]{3,2,1,0:T(8,128)(2,1)}, u32[]{:S(2)}) %copy-start) | copy-done | bytes 1310744
  2.9 0.0 copy-start.1
  2.9 0.8 %copy-done.1 = f32[2,32,128]{2,1,0:T(8,128)S(1)} copy-done((f32[2,32,128]{2,1,0:T(8,128)S(1)}, f32[2,32,128]{2,1,0:T(8,128)}, u32[]{:S(2)}) %copy-start.1) | copy-done | bytes 32792
  3.7 51.2 %shard_map.46 = f32[2,32,128]{2,1,0:T(8,128)S(1)} custom-call(bf16[80,2,32,128]{3,2,1,0:T(8,128)(2,1)S(1)} %copy-done, f32[2,32,128]{2,1,0:T(8,128)S(1)} %copy-done.1, f32[1,1024]{1,0:T(1,128)S(1)} %bitcast.3, f32[1,256]{1,0:T(1,128)S(1)} %bitcast.4), custom_call_target="tpu_custom_call" | custom-call | tf_op jit(solution)/shard_map/pallas_call | solution.py:251
  54.9 0.6 %copy.6 = f32[2,32,128]{2,1,0:T(8,128)} copy(f32[2,32,128]{2,1,0:T(8,128)S(1)} %shard_map.46) | data formatting | bytes 65536
Async XLA Ops:
  1.6 1.3 %copy-start = (bf16[80,2,32,128]{3,2,1,0:T(8,128)(2,1)S(1)}, bf16[80,2,32,128]{3,2,1,0:T(8,128)(2,1)}, u32[]{:S(2)}) copy-start(bf16[80,2,32,128]{3,2,1,0:T(8,128)(2,1)} %members.1) | copy-start | bytes 3932164
  2.9 0.8 %copy-start.1 = (f32[2,32,128]{2,1,0:T(8,128)S(1)}, f32[2,32,128]{2,1,0:T(8,128)}, u32[]{:S(2)}) copy-start(f32[2,32,128]{2,1,0:T(8,128)} %gradient.1) | copy-start | bytes 98308

commit v2 on v0

--- a/solution.py
+++ b/solution.py
@@ -1,7 +1,14 @@
+import functools
+
 import jax
 import jax.numpy as jnp
 from jax import lax
+from jax.experimental import pallas as pl
+from jax.experimental.pallas import tpu as pltpu
 from jax.sharding import PartitionSpec as P
+
+MESH = pl.DeviceIdType.MESH
+VMEM_BYTES = 60 * 1024 * 1024
 
 
 def from_behind(value, axis, steps):
@@ -40,7 +47,7 @@
     return jnp.concatenate([pieces[2], pieces[1], values, pieces[-1], pieces[-2]], axis=2)
 
 
-def per_device(members, gradient, lon_taper, lat_taper):
+def halo_plan(members, gradient, lon_taper, lat_taper):
     clat = gradient.shape[1]
     clon = gradient.shape[2]
     count = members.shape[0]
@@ -57,6 +64,260 @@
     return weighted / (count - 1)
 
 
+def member_kernel(
+    n_lon, n_lat, count,
+    members, gradient, lines, out,
+    grad_z, grad_all, taken, stack, along, total, lon_table, lat_table, partial, parts,
+    gz_send, gz_recv, own_grad, ga_send, ga_recv, m_send, m_recv, r_send, r_recv,
+):
+    i, j = lax.axis_index("lon"), lax.axis_index("lat")
+    clat, clon = gradient.shape[1], gradient.shape[2]
+    n = n_lon * n_lat
+    share = taken.shape[0]
+    lat_cells = n_lat * clat
+    pairs = n_lon // 2
+    level = lax.rem(i, 2)
+    place = (i // 2) * n_lat + j
+
+    def other(k):
+        i_to = lax.rem(i + k // n_lat, n_lon)
+        j_to = lax.rem(j + lax.rem(k, n_lat), n_lat)
+        return i_to, j_to
+
+    def lat_rows(j_at):
+        return pl.ds(pl.multiple_of(j_at * clat, clat), clat)
+
+    barrier = pltpu.get_barrier_semaphore()
+
+    def greet(k, c):
+        i_to, j_to = other(k)
+        pl.semaphore_signal(barrier, inc=1, device_id={"lon": i_to, "lat": j_to}, device_id_type=MESH)
+        return c
+
+    lax.fori_loop(1, n, greet, 0)
+
+    own = pltpu.make_async_copy(gradient, grad_z.at[j], own_grad)
+    own.start()
+    for m in range(share):
+        pltpu.make_async_copy(
+            members.at[place * share + m, level], taken.at[m, i, lat_rows(j), :], m_recv.at[m]
+        ).start()
+
+    rows, cols = lon_table.shape
+    line = 8 * clon
+    spread = jnp.broadcast_to(lines[:, :line], (rows, line))
+    turned = pltpu.roll(spread, line - 6 * clon, 1, stride=1, stride_axis=0)
+    lon_table[...] = turned[:, :cols].astype(jnp.bfloat16)
+    spread = jnp.broadcast_to(lines[:, line:], (lat_cells, 2 * lat_cells))
+    turned = pltpu.roll(spread, lat_cells, 1, stride=1, stride_axis=0)
+    lat_table[...] = turned[:, :lat_cells].T.astype(jnp.bfloat16)
+
+    pl.semaphore_wait(barrier, n - 1)
+    own.wait()
+
+    def grad_z_copies(s):
+        up = pltpu.make_async_remote_copy(
+            src_ref=grad_z.at[lax.max(j - s, 0)], dst_ref=grad_z.at[lax.max(j - s, 0)],
+            send_sem=gz_send.at[0, s], recv_sem=gz_recv.at[0, s],
+            device_id={"lon": i, "lat": lax.min(j + 1, n_lat - 1)}, device_id_type=MESH,
+        )
+        down = pltpu.make_async_remote_copy(
+            src_ref=grad_z.at[lax.min(j + s, n_lat - 1)], dst_ref=grad_z.at[lax.min(j + s, n_lat - 1)],
+            send_sem=gz_send.at[1, s], recv_sem=gz_recv.at[1, s],
+            device_id={"lon": i, "lat": lax.max(j - 1, 0)}, device_id_type=MESH,
+        )
+        return up, down
+
+    def grad_z_start(s):
+        up, down = grad_z_copies(s)
+
+        @pl.when((j - s >= 0) & (j + 1 < n_lat))
+        def _():
+            up.start()
+
+        @pl.when((j + s < n_lat) & (j - 1 >= 0))
+        def _():
+            down.start()
+
+    def grad_z_wait(s):
+        up, down = grad_z_copies(s)
+
+        @pl.when((j - s >= 0) & (j + 1 < n_lat))
+        def _():
+            up.wait_send()
+
+        @pl.when((j + s < n_lat) & (j - 1 >= 0))
+        def _():
+            down.wait_send()
+
+        @pl.when(j - 1 - s >= 0)
+        def _():
+            pltpu.make_async_remote_copy(
+                src_ref=grad_z.at[0], dst_ref=grad_z.at[lax.max(j - 1 - s, 0)],
+                send_sem=gz_send.at[0, s], recv_sem=gz_recv.at[0, s],
+                device_id={"lon": i, "lat": lax.max(j - 1, 0)}, device_id_type=MESH,
+            ).wait_recv()
+
+        @pl.when(j + 1 + s < n_lat)
+        def _():
+            pltpu.make_async_remote_copy(
+                src_ref=grad_z.at[0], dst_ref=grad_z.at[lax.min(j + 1 + s, n_lat - 1)],
+                send_sem=gz_send.at[1, s], recv_sem=gz_recv.at[1, s],
+                device_id={"lon": i, "lat": lax.min(j + 1, n_lat - 1)}, device_id_type=MESH,
+            ).wait_recv()
+
+    def start_members(m):
+        def start(k, c):
+            i_to, j_to = other(k)
+            at = ((i_to // 2) * n_lat + j_to) * share + m
+            pltpu.make_async_remote_copy(
+                src_ref=members.at[at, lax.rem(i_to, 2)], dst_ref=taken.at[m, i, lat_rows(j), :],
+                send_sem=m_send.at[m], recv_sem=m_recv.at[m],
+                device_id={"lon": i_to, "lat": j_to}, device_id_type=MESH,
+            ).start()
+            return c
+
+        lax.fori_loop(1, n, start, 0)
+
+    sent = members.at[pl.ds(0, n - 1), 0]
+
+    def wait_members(m):
+        pltpu.make_async_copy(taken.at[m], taken.at[m], m_recv.at[m]).wait()
+        pltpu.make_async_copy(sent, sent, m_send.at[m]).wait()
+
+    def grad_all_copy(k):
+        i_to = lax.rem(i + k, n_lon)
+        return pltpu.make_async_remote_copy(
+            src_ref=grad_z.at[:, lax.rem(i_to, 2)], dst_ref=grad_all.at[i],
+            send_sem=ga_send.at[i_to], recv_sem=ga_recv.at[i],
+            device_id={"lon": i_to, "lat": j}, device_id_type=MESH,
+        )
+
+    grad_z_start(0)
+    started = 0
+    for s in range(n_lat - 1):
+        if started < share:
+            start_members(started)
+            started += 1
+        grad_z_wait(s)
+        if s + 1 < n_lat - 1:
+            grad_z_start(s + 1)
+    for k in range(1, n_lon):
+        grad_all_copy(k).start()
+    for m in range(started, share):
+        start_members(m)
+    grad_all[i] = grad_z[:, level]
+    for k in range(1, n_lon):
+        i_from = lax.rem(i + k, n_lon)
+        pltpu.make_async_remote_copy(
+            src_ref=grad_z.at[:, 0], dst_ref=grad_all.at[i_from],
+            send_sem=ga_send.at[i_from], recv_sem=ga_recv.at[i_from],
+            device_id={"lon": i_from, "lat": j}, device_id_type=MESH,
+        ).wait()
+
+    def pair_term(m, o, along_lon):
+        along_lat = jnp.dot(lat_table[...], along_lon, preferred_element_type=jnp.float32)
+        x = jnp.concatenate([taken[m, 2 * o], taken[m, 2 * o + 1]], axis=1)
+        return x.astype(jnp.float32) * along_lat
+
+    def part_copy(i_to, j_to):
+        return pltpu.make_async_remote_copy(
+            src_ref=partial.at[i_to, lat_rows(j_to), :], dst_ref=parts.at[level, place],
+            send_sem=r_send, recv_sem=r_recv,
+            device_id={"lon": i_to, "lat": j_to}, device_id_type=MESH,
+        )
+
+    for m in range(share):
+        wait_members(m)
+        for b in range(n_lon):
+            g = grad_all[b].reshape(lat_cells, clon)
+            p = (taken[m, b].astype(jnp.float32) * g).astype(jnp.bfloat16)
+            for step in (-1, 0, 1):
+                o = (b // 2 + step) % pairs
+                at = (b % 2 + 2 - 2 * step) * clon
+                stack[o * lat_cells:(o + 1) * lat_cells, at:at + clon] = p
+        along_lon = jnp.dot(
+            stack[...], lon_table[...], preferred_element_type=jnp.float32
+        ).astype(jnp.bfloat16)
+        if m < share - 1:
+            for o in range(pairs):
+                term = pair_term(m, o, along_lon[o * lat_cells:(o + 1) * lat_cells])
+                total[o] = term if m == 0 else total[o] + term
+            continue
+        along[...] = along_lon
+        for t in range(pairs):
+            o = lax.rem(i // 2 + 1 + t, pairs)
+            window = along[pl.ds(pl.multiple_of(o * lat_cells, lat_cells), lat_cells), :]
+            done = pair_term(m, o, window)
+            if share > 1:
+                done += total[o]
+            for c in range(2):
+                partial[2 * o + c] = done[:, c * clon:(c + 1) * clon].astype(jnp.bfloat16)
+            for c in range(2):
+                for k in range(n_lat):
+                    j_to = lax.rem(j + 1 + k, n_lat)
+                    if t < pairs - 1 or k < n_lat - 1:
+                        part_copy(2 * o + c, j_to).start()
+                    else:
+                        @pl.when(c != level)
+                        def _():
+                            part_copy(2 * o + c, j_to).start()
+
+    kept = pltpu.make_async_copy(partial.at[i, lat_rows(j), :], parts.at[level, place], r_recv)
+    kept.start()
+    pltpu.make_async_copy(parts, parts, r_recv).wait()
+    for l in range(2):
+        out[l] = jnp.sum(parts[l].astype(jnp.float32), axis=0) / (count - 1)
+    pltpu.make_async_copy(sent, sent, r_send).wait()
+
+
+def member_plan(members, gradient, lon_taper, lat_taper):
+    n_lon, n_lat = lax.axis_size("lon"), lax.axis_size("lat")
+    count, levels, clat, clon = members.shape
+    share = count // (n_lon // 2 * n_lat)
+    lat_cells = n_lat * clat
+    side = lat_cells - 2 * clat
+    lines = jnp.concatenate([
+        jnp.pad(lon_taper, (2 * clon, 2 * clon - 1)), jnp.pad(lat_taper, (side, side - 1))
+    ]).astype(jnp.float32)[None]
+    n = n_lon * n_lat
+    vmem = pl.BlockSpec(memory_space=pltpu.VMEM)
+    hbm = pl.BlockSpec(memory_space=pl.ANY)
+    dma = pltpu.SemaphoreType.DMA
+    return pl.pallas_call(
+        functools.partial(member_kernel, n_lon, n_lat, count),
+        out_shape=jax.ShapeDtypeStruct(gradient.shape, jnp.float32),
+        in_specs=[hbm, hbm, vmem],
+        out_specs=vmem,
+        scratch_shapes=[
+            pltpu.VMEM((n_lat, levels, clat, clon), jnp.float32),
+            pltpu.VMEM((n_lon, n_lat, clat, clon), jnp.float32),
+            pltpu.VMEM((share, n_lon, lat_cells, clon), jnp.bfloat16),
+            pltpu.VMEM((n_lon // 2 * lat_cells, 6 * clon), jnp.bfloat16),
+            pltpu.VMEM((n_lon // 2 * lat_cells, 2 * clon), jnp.bfloat16),
+            pltpu.VMEM((n_lon // 2, lat_cells, 2 * clon), jnp.float32),
+            pltpu.VMEM((6 * clon, 2 * clon), jnp.bfloat16),
+            pltpu.VMEM((lat_cells, lat_cells), jnp.bfloat16),
+            pltpu.VMEM((n_lon, lat_cells, clon), jnp.bfloat16),
+            pltpu.VMEM((2, n // 2, clat, clon), jnp.bfloat16),
+            dma((2, n_lat)), dma((2, n_lat)), dma, dma((n_lon,)), dma((n_lon,)),
+            dma((share,)), dma((share,)), dma, dma,
+        ],
+        compiler_params=pltpu.CompilerParams(
+            collective_id=0, has_side_effects=True, vmem_limit_bytes=VMEM_BYTES
+        ),
+    )(members, gradient, lines)
+
+
+def per_device(members, gradient, lon_taper, lat_taper):
+    n_lon, n_lat = lax.axis_size("lon"), lax.axis_size("lat")
+    count, levels, clat, clon = members.shape
+    even = levels == 2 and n_lon % 2 == 0 and n_lon >= 6
+    if even and count % (n_lon // 2 * n_lat) == 0 and n_lat * clat % 128 == 0 and n_lat >= 3 and count >= n_lon * n_lat:
+        return member_plan(members, gradient, lon_taper, lat_taper)
+    return halo_plan(members, gradient, lon_taper, lat_taper)
+
+
 def solution(mesh):
     in_specs = (P(None, None, "lat", "lon"), P(None, "lat", "lon"), P(), P())
     out_specs = P(None, "lat", "lon")

time: 620 us -> 51.9 us (0.08)
  local copies, waits for them, and re-layouts: 545 us -> 2.81 us
  Pallas kernels: 0 us -> 48.2 us
  waiting for transfers between devices: 48.2 us -> 0 us
  starting transfers between devices: 18.8 us -> 0 us
    gather x3 -> x0, local copies, waits for them, and re-layouts: 533 us -> none  [taper_table(): picked = jnp.take(weights, where_at, axis=0)]
    ppermute x8 -> x0, waiting for transfers between devices: 48.2 us -> none  [the longest x4 48.2 us: from_behind_2(): return lax.ppermute(block, axis, route)]
    pallas_call x0 -> x1, Pallas kernels: none -> 48.2 us  [member_plan(): pl.pallas_call(functools.partial(member_kernel, n_lon, n_lat, count), out...]
    ppermute x8 -> x0, starting transfers between devices: 18.8 us -> none  [the longest x4 13.1 us: from_behind_2(): return lax.ppermute(block, axis, route)]
    unnamed x15 -> x1, local copies, waits for them, and re-layouts: 10.3 us -> 1.38 us
  transfers between devices with their start and end apart: 8 -> 0, of which waited for: 2 -> 0; matrix products, arithmetic and copies ran while one was open for 88% -> 0% of each run, Pallas kernels for 0% -> 0%
where the time goes in v2:
time: 51.9 us; the launch traced here: 51.6 us
  Pallas kernels  48.2 us (93%)
  local copies, waits for them, and re-layouts  2.81 us (5%)
  other arithmetic  0.6 us (1%)
    pallas_call x1, Pallas kernels, member_plan(): pl.pallas_call(functools.partial(member_kernel, n_lon, n_lat, count), out...  48.2 us
    unnamed x1, local copies, waits for them, and re-layouts  1.38 us

profile of v2, /device:TPU:0, one launch (start us, length us, event | category | flops | bytes accessed | tf_op | source)
XLA Modules:
  0.0 51.6 jit_solution(7691753280060434142)
XLA Ops:
  0.0 0.7 %pad.9 = bf16[256]{0:T(256)(128)(2,1)S(1)} pad(bf16[129]{0:T(256)(128)(2,1)} %param.7, bf16[]{:T(256)} %constant.2.clone.1), padding=64_63 | pad | bytes 772 | tf_op jit(solution)/shard_map/jit(_pad)/pad | solution.py:281
  0.7 0.7 %pad.8 = bf16[1024]{0:T(1024)(128)(2,1)S(1)} pad(bf16[513]{0:T(1024)(128)(2,1)} %param.6, bf16[]{:T(256)} %constant.2.clone.1), padding=256_255 | pad | bytes 3076 | tf_op jit(solution)/shard_map/jit(_pad)/pad | solution.py:281
  1.4 0.6 %maximum_convert_fusion.lines = f32[1,1280]{1,0:T(1,128)} fusion(bf16[1,256]{1,0:T(2,128)(2,1)S(1)} %concatenate.15, bf16[1,1024]{1,0:T(2,128)(2,1)S(1)} %concatenate.14), kind=kLoop, calls=%fused_computation | loop fusion | flops 5120 | bytes 7680 | tf_op jit(solution)/shard_map/convert_element_type | solution.py:282
  2.0 48.2 %shard_map.46 = f32[2,32,128]{2,1,0:T(8,128)} custom-call(bf16[80,2,32,128]{3,2,1,0:T(8,128)(2,1)} %members.1, f32[2,32,128]{2,1,0:T(8,128)} %gradient.1, f32[1,1280]{1,0:T(1,128)} %maximum_convert_fusion.lines), custom_call_target="tpu_custom_call" | custom-call | tf_op jit(solution)/shard_map/pallas_call | solution.py:287
  50.2 1.4 %copy.6 = f32[2,32,128]{2,1,0:T(8,128)} copy(f32[2,32,128]{2,1,0:T(8,128)} %shard_map.46) | data formatting | bytes 65536
  (2 shorter events, 0.0 us)

commit v3 on v2

--- a/solution.py
+++ b/solution.py
@@ -66,9 +66,9 @@
 
 def member_kernel(
     n_lon, n_lat, count,
-    members, gradient, lines, out,
-    grad_z, grad_all, taken, stack, along, total, lon_table, lat_table, partial, parts,
-    gz_send, gz_recv, own_grad, ga_send, ga_recv, m_send, m_recv, r_send, r_recv,
+    members, gradient, lon_taper, lat_taper, out,
+    lon_line, lat_line, grad_z, grad_all, taken, stack, along, total, lon_table, lat_table, partial, parts,
+    line_sem, gz_send, gz_recv, own_grad, ga_send, ga_recv, m_send, m_recv, r_send, r_recv,
 ):
     i, j = lax.axis_index("lon"), lax.axis_index("lat")
     clat, clon = gradient.shape[1], gradient.shape[2]
@@ -87,6 +87,11 @@
     def lat_rows(j_at):
         return pl.ds(pl.multiple_of(j_at * clat, clat), clat)
 
+    lon_in = pltpu.make_async_copy(lon_taper, lon_line, line_sem.at[0])
+    lat_in = pltpu.make_async_copy(lat_taper, lat_line, line_sem.at[1])
+    lon_in.start()
+    lat_in.start()
+
     barrier = pltpu.get_barrier_semaphore()
 
     def greet(k, c):
@@ -103,12 +108,19 @@
             members.at[place * share + m, level], taken.at[m, i, lat_rows(j), :], m_recv.at[m]
         ).start()
 
+    def centred(values, length):
+        values = values.astype(jnp.float32).reshape(1, values.shape[0])
+        side = (length - values.shape[1] + 1) // 2
+        return jnp.pad(values, ((0, 0), (side, side - 1)))
+
+    lon_in.wait()
+    lat_in.wait()
     rows, cols = lon_table.shape
     line = 8 * clon
-    spread = jnp.broadcast_to(lines[:, :line], (rows, line))
+    spread = jnp.broadcast_to(centred(lon_line[...], line), (rows, line))
     turned = pltpu.roll(spread, line - 6 * clon, 1, stride=1, stride_axis=0)
     lon_table[...] = turned[:, :cols].astype(jnp.bfloat16)
-    spread = jnp.broadcast_to(lines[:, line:], (lat_cells, 2 * lat_cells))
+    spread = jnp.broadcast_to(centred(lat_line[...], 2 * lat_cells), (lat_cells, 2 * lat_cells))
     turned = pltpu.roll(spread, lat_cells, 1, stride=1, stride_axis=0)
     lat_table[...] = turned[:, :lat_cells].T.astype(jnp.bfloat16)
 
@@ -168,16 +180,21 @@
 
     def start_members(m):
         def start(k, c):
-            i_to, j_to = other(k)
+            i_to = lax.rem(i + lax.rem(k, n_lon), n_lon)
+            j_to = lax.rem(j // 2 * 2 + 2 + k // n_lon, n_lat)
             at = ((i_to // 2) * n_lat + j_to) * share + m
-            pltpu.make_async_remote_copy(
-                src_ref=members.at[at, lax.rem(i_to, 2)], dst_ref=taken.at[m, i, lat_rows(j), :],
-                send_sem=m_send.at[m], recv_sem=m_recv.at[m],
-                device_id={"lon": i_to, "lat": j_to}, device_id_type=MESH,
-            ).start()
+
+            @pl.when((i_to != i) | (j_to != j))
+            def _():
+                pltpu.make_async_remote_copy(
+                    src_ref=members.at[at, lax.rem(i_to, 2)], dst_ref=taken.at[m, i, lat_rows(j), :],
+                    send_sem=m_send.at[m], recv_sem=m_recv.at[m],
+                    device_id={"lon": i_to, "lat": j_to}, device_id_type=MESH,
+                ).start()
+
             return c
 
-        lax.fori_loop(1, n, start, 0)
+        lax.fori_loop(0, n, start, 0)
 
     sent = members.at[pl.ds(0, n - 1), 0]
 
@@ -253,13 +270,13 @@
                 done += total[o]
             for c in range(2):
                 partial[2 * o + c] = done[:, c * clon:(c + 1) * clon].astype(jnp.bfloat16)
-            for c in range(2):
-                for k in range(n_lat):
-                    j_to = lax.rem(j + 1 + k, n_lat)
-                    if t < pairs - 1 or k < n_lat - 1:
+            for k in range(n_lat):
+                j_to = lax.rem(j // 2 * 2 + 2 + k, n_lat)
+                for c in range(2):
+                    if t < pairs - 1:
                         part_copy(2 * o + c, j_to).start()
                     else:
-                        @pl.when(c != level)
+                        @pl.when((c != level) | (j_to != j))
                         def _():
                             part_copy(2 * o + c, j_to).start()
 
@@ -276,20 +293,18 @@
     count, levels, clat, clon = members.shape
     share = count // (n_lon // 2 * n_lat)
     lat_cells = n_lat * clat
-    side = lat_cells - 2 * clat
-    lines = jnp.concatenate([
-        jnp.pad(lon_taper, (2 * clon, 2 * clon - 1)), jnp.pad(lat_taper, (side, side - 1))
-    ]).astype(jnp.float32)[None]
     n = n_lon * n_lat
     vmem = pl.BlockSpec(memory_space=pltpu.VMEM)
     hbm = pl.BlockSpec(memory_space=pl.ANY)
     dma = pltpu.SemaphoreType.DMA
     return pl.pallas_call(
         functools.partial(member_kernel, n_lon, n_lat, count),
-        out_shape=jax.ShapeDtypeStruct(gradient.shape, jnp.float32),
-        in_specs=[hbm, hbm, vmem],
+        out_shape=pltpu.VMEM(gradient.shape, jnp.float32),
+        in_specs=[hbm, hbm, hbm, hbm],
         out_specs=vmem,
         scratch_shapes=[
+            pltpu.VMEM(lon_taper.shape, lon_taper.dtype),
+            pltpu.VMEM(lat_taper.shape, lat_taper.dtype),
             pltpu.VMEM((n_lat, levels, clat, clon), jnp.float32),
             pltpu.VMEM((n_lon, n_lat, clat, clon), jnp.float32),
             pltpu.VMEM((share, n_lon, lat_cells, clon), jnp.bfloat16),
@@ -300,13 +315,13 @@
             pltpu.VMEM((lat_cells, lat_cells), jnp.bfloat16),
             pltpu.VMEM((n_lon, lat_cells, clon), jnp.bfloat16),
             pltpu.VMEM((2, n // 2, clat, clon), jnp.bfloat16),
-            dma((2, n_lat)), dma((2, n_lat)), dma, dma((n_lon,)), dma((n_lon,)),
+            dma((2,)), dma((2, n_lat)), dma((2, n_lat)), dma, dma((n_lon,)), dma((n_lon,)),
             dma((share,)), dma((share,)), dma, dma,
         ],
         compiler_params=pltpu.CompilerParams(
             collective_id=0, has_side_effects=True, vmem_limit_bytes=VMEM_BYTES
         ),
-    )(members, gradient, lines)
+    )(members, gradient, lon_taper, lat_taper)
 
 
 def per_device(members, gradient, lon_taper, lat_taper):

time: 51.9 us -> 47.3 us (0.911)
  local copies, waits for them, and re-layouts: 2.81 us -> 0.62 us
  Pallas kernels: 48.2 us -> 46.5 us
  other arithmetic: 0.6 us -> 0 us
    pallas_call x1, Pallas kernels: 48.2 us -> 46.5 us  [member_plan(): pl.pallas_call(functools.partial(member_kernel, n_lon, n_lat, count), out...]
    pad x2 -> x0, local copies, waits for them, and re-layouts: 1.42 us -> none  [the longest x1 0.73 us: member_plan(): jnp.pad(lat_taper, (side, side - 1))]
    unnamed x1, local copies, waits for them, and re-layouts: 1.38 us -> 0.62 us
    convert_element_type x1 -> x0, other arithmetic: 0.6 us -> none  [member_plan(): lines = jnp.concatenate([jnp.pad(lon_taper, (2 * clon, 2 * clon - 1)), jn...]
where the time goes in v3:
time: 47.3 us; the launch traced here: 47.2 us
  Pallas kernels  46.5 us (98%)
  local copies, waits for them, and re-layouts  0.62 us (1%)
    pallas_call x1, Pallas kernels, member_plan(): pl.pallas_call(functools.partial(member_kernel, n_lon, n_lat, count), out...  46.5 us

profile of v3, /device:TPU:0, one launch (start us, length us, event | category | flops | bytes accessed | tf_op | source)
XLA Modules:
  0.0 47.2 jit_solution(4051001506556588689)
XLA Ops:
  0.0 46.5 %shard_map.46 = f32[2,32,128]{2,1,0:T(8,128)S(1)} custom-call(bf16[80,2,32,128]{3,2,1,0:T(8,128)(2,1)} %members.1, f32[2,32,128]{2,1,0:T(8,128)} %gradient.1, bf16[513]{0:T(1024)(128)(2,1)} %lon_taper.1, bf16[129]{0:T(256)(128)(2,1)} %lat_taper.1), custom_call_target="tpu_custom_call" | custom-call | tf_op jit(solution)/shard_map/pallas_call | solution.py:300
  46.5 0.6 %copy.6 = f32[2,32,128]{2,1,0:T(8,128)} copy(f32[2,32,128]{2,1,0:T(8,128)S(1)} %shard_map.46) | data formatting | bytes 65536

commit v4 on v0

--- a/solution.py
+++ b/solution.py
@@ -1,7 +1,15 @@
+import functools
+
 import jax
 import jax.numpy as jnp
 from jax import lax
+from jax.experimental import pallas as pl
+from jax.experimental.pallas import tpu as pltpu
 from jax.sharding import PartitionSpec as P
+
+MESH = pl.DeviceIdType.MESH
+VMEM_BYTES = 60 * 1024 * 1024
+CHUNK = 2
 
 
 def from_behind(value, axis, steps):
@@ -40,7 +48,7 @@
     return jnp.concatenate([pieces[2], pieces[1], values, pieces[-1], pieces[-2]], axis=2)
 
 
-def per_device(members, gradient, lon_taper, lat_taper):
+def halo_plan(members, gradient, lon_taper, lat_taper):
     clat = gradient.shape[1]
     clon = gradient.shape[2]
     count = members.shape[0]
@@ -57,6 +65,290 @@
     return weighted / (count - 1)
 
 
+def member_kernel(
+    n_lon, n_lat, count,
+    members, gradient, lon_taper, lat_taper, out,
+    lon_line, lat_line, grad_z, grad_all, taken, stack, along, total, lon_table, lat_table, partial, parts,
+    line_sem, gz_send, gz_recv, own_grad, ga_send, ga_recv, m_send, m_recv, r_send, r_recv,
+):
+    i, j = lax.axis_index("lon"), lax.axis_index("lat")
+    clat, clon = gradient.shape[1], gradient.shape[2]
+    n = n_lon * n_lat
+    share = taken.shape[0]
+    half = j // 2
+    beside = 2 - half
+    mate = 4 * half + 1 - j
+    outer = (j == 0) | (j == n_lat - 1)
+    frame = taken.shape[2]
+    pairs = n_lon // 2
+    level = lax.rem(i, 2)
+    place = (i // 2) * 2 + lax.rem(j, 2)
+
+    def other(k):
+        i_to = lax.rem(i + k // n_lat, n_lon)
+        j_to = lax.rem(j + lax.rem(k, n_lat), n_lat)
+        return i_to, j_to
+
+    def frame_rows(j_at, in_half):
+        return pl.ds(pl.multiple_of((j_at - in_half) * clat, clat), clat)
+
+    lon_in = pltpu.make_async_copy(lon_taper, lon_line, line_sem.at[0])
+    lat_in = pltpu.make_async_copy(lat_taper, lat_line, line_sem.at[1])
+    lon_in.start()
+    lat_in.start()
+
+    barrier = pltpu.get_barrier_semaphore()
+
+    def greet(k, c):
+        i_to, j_to = other(k)
+        pl.semaphore_signal(barrier, inc=1, device_id={"lon": i_to, "lat": j_to}, device_id_type=MESH)
+        return c
+
+    lax.fori_loop(1, n, greet, 0)
+
+    own = pltpu.make_async_copy(gradient, grad_z.at[j - half], own_grad)
+    own.start()
+    for q in range(share // CHUNK):
+        pltpu.make_async_copy(
+            members.at[pl.ds(place * share + q * CHUNK, CHUNK), level],
+            taken.at[pl.ds(q * CHUNK, CHUNK), i, frame_rows(j, half), :], m_recv.at[q],
+        ).start()
+
+    def centred(values, length):
+        values = values.astype(jnp.float32).reshape(1, values.shape[0])
+        side = (length - values.shape[1] + 1) // 2
+        return jnp.pad(values, ((0, 0), (side, side - 1)))
+
+    lon_in.wait()
+    lat_in.wait()
+    rows, cols = lon_table.shape
+    line = 8 * clon
+    spread = jnp.broadcast_to(centred(lon_line[...], line), (rows, line))
+    turned = pltpu.roll(spread, line - 6 * clon, 1, stride=1, stride_axis=0)
+    lon_table[...] = turned[:, :cols].astype(jnp.bfloat16)
+    lat_line_cells = 8 * clat
+    spread = jnp.broadcast_to(centred(lat_line[...], lat_line_cells), (4 * clat, lat_line_cells))
+    turned = pltpu.roll(spread, 4 * clat, 1, stride=1, stride_axis=0)
+    whole = turned[:, :4 * clat].T[:frame, :frame]
+    to_block = lax.broadcasted_iota(jnp.int32, (frame, frame), 0) // clat
+    from_block = lax.broadcasted_iota(jnp.int32, (frame, frame), 1) // clat
+    kept_here = (to_block != 2 - 2 * half) | (from_block == 2 * half)
+    lat_table[...] = jnp.where(kept_here, whole, 0.0).astype(jnp.bfloat16)
+
+    pl.semaphore_wait(barrier, n - 1)
+    own.wait()
+
+    def grad_z_copy(j_to, slot):
+        return pltpu.make_async_remote_copy(
+            src_ref=gradient, dst_ref=grad_z.at[j - j_to // 2],
+            send_sem=gz_send.at[slot], recv_sem=gz_recv.at[j - j_to // 2],
+            device_id={"lon": i, "lat": j_to}, device_id_type=MESH,
+        )
+
+    across = 2 - 2 * half
+
+    def start_members(q):
+        def to_half(first):
+            def start(k, c):
+                i_to = lax.rem(i + lax.rem(k, n_lon), n_lon)
+                j_to = first + lax.rem(j + k // n_lon, 2)
+                at = ((i_to // 2) * 2 + lax.rem(j_to, 2)) * share + q * CHUNK
+
+                @pl.when((i_to != i) | (j_to != j))
+                def _():
+                    pltpu.make_async_remote_copy(
+                        src_ref=members.at[pl.ds(at, CHUNK), lax.rem(i_to, 2)],
+                        dst_ref=taken.at[pl.ds(q * CHUNK, CHUNK), i, frame_rows(j, first // 2), :],
+                        send_sem=m_send.at[q], recv_sem=m_recv.at[q],
+                        device_id={"lon": i_to, "lat": j_to}, device_id_type=MESH,
+                    ).start()
+
+                return c
+
+            lax.fori_loop(0, 2 * n_lon, start, 0)
+
+        @pl.when(jnp.logical_not(outer))
+        def _():
+            to_half(across)
+
+        to_half(2 * half)
+
+    def wait_blocks(count, sem):
+        sent = members.at[pl.ds(0, count), 0]
+        pltpu.make_async_copy(sent, sent, sem).wait()
+
+    def wait_members(q):
+        here = taken.at[pl.ds(q * CHUNK, CHUNK)]
+        pltpu.make_async_copy(here, here, m_recv.at[q]).wait()
+        wait_blocks((n // 2 - 1) * CHUNK, m_send.at[q])
+
+        @pl.when(jnp.logical_not(outer))
+        def _():
+            wait_blocks(n // 2 * CHUNK, m_send.at[q])
+
+    def grad_all_copy(k):
+        i_to = lax.rem(i + k, n_lon)
+        return pltpu.make_async_remote_copy(
+            src_ref=grad_z.at[:, lax.rem(i_to, 2)], dst_ref=grad_all.at[i],
+            send_sem=ga_send.at[i_to], recv_sem=ga_recv.at[i],
+            device_id={"lon": i_to, "lat": j}, device_id_type=MESH,
+        )
+
+    @pl.when(jnp.logical_not(outer))
+    def _():
+        for c in range(2):
+            grad_z_copy(across + c, 1 + c).start()
+
+    grad_z_copy(mate, 0).start()
+    start_members(0)
+    grad_z_copy(mate, 0).wait_send()
+
+    @pl.when(jnp.logical_not(outer))
+    def _():
+        for c in range(2):
+            grad_z_copy(across + c, 1 + c).wait_send()
+
+    for j_from in (mate, beside):
+        pltpu.make_async_remote_copy(
+            src_ref=gradient, dst_ref=grad_z.at[j_from - half],
+            send_sem=gz_send.at[0], recv_sem=gz_recv.at[j_from - half],
+            device_id={"lon": i, "lat": j_from}, device_id_type=MESH,
+        ).wait_recv()
+    for k in range(1, n_lon):
+        grad_all_copy(k).start()
+    for q in range(1, share // CHUNK):
+        start_members(q)
+    grad_all[i] = grad_z[:, level]
+    for k in range(1, n_lon):
+        i_from = lax.rem(i + k, n_lon)
+        pltpu.make_async_remote_copy(
+            src_ref=grad_z.at[:, 0], dst_ref=grad_all.at[i_from],
+            send_sem=ga_send.at[i_from], recv_sem=ga_recv.at[i_from],
+            device_id={"lon": i_from, "lat": j}, device_id_type=MESH,
+        ).wait()
+
+    def pair_term(m, o, along_lon):
+        along_lat = jnp.dot(lat_table[...], along_lon, preferred_element_type=jnp.float32)
+        x = jnp.concatenate([taken[m, 2 * o], taken[m, 2 * o + 1]], axis=1)
+        return x.astype(jnp.float32) * along_lat
+
+    def part_copy(i_to, j_to, crosses):
+        return pltpu.make_async_remote_copy(
+            src_ref=partial.at[i_to, frame_rows(j_to, half), :], dst_ref=parts.at[crosses, level, place],
+            send_sem=r_send, recv_sem=r_recv,
+            device_id={"lon": i_to, "lat": j_to}, device_id_type=MESH,
+        )
+
+    span = CHUNK * frame
+    for q in range(share // CHUNK):
+        wait_members(q)
+        for b in range(n_lon):
+            g = grad_all[b].reshape(frame, clon)
+            for e in range(CHUNK):
+                p = (taken[q * CHUNK + e, b].astype(jnp.float32) * g).astype(jnp.bfloat16)
+                for step in (-1, 0, 1):
+                    o = (b // 2 + step) % pairs
+                    at = (b % 2 + 2 - 2 * step) * clon
+                    row = o * span + e * frame
+                    stack[row:row + frame, at:at + clon] = p
+        along_lon = jnp.dot(
+            stack[...], lon_table[...], preferred_element_type=jnp.float32
+        ).astype(jnp.bfloat16)
+        if q < share // CHUNK - 1:
+            for o in range(pairs):
+                for e in range(CHUNK):
+                    row = o * span + e * frame
+                    term = pair_term(q * CHUNK + e, o, along_lon[row:row + frame])
+                    total[o] = term if q + e == 0 else total[o] + term
+            continue
+        along[...] = along_lon
+        for t in range(pairs):
+            o = lax.rem(i // 2 + 1 + t, pairs)
+            done = total[o]
+            for e in range(CHUNK):
+                row = pl.multiple_of(o * span + e * frame, clat)
+                done += pair_term(q * CHUNK + e, o, along[pl.ds(row, frame), :])
+            for c in range(2):
+                partial[2 * o + c] = done[:, c * clon:(c + 1) * clon].astype(jnp.bfloat16)
+            for c in range(2):
+                part_copy(2 * o + c, beside, 1).start()
+            for c in range(2):
+                part_copy(2 * o + c, mate, 0).start()
+            for c in range(2):
+                if t < pairs - 1:
+                    part_copy(2 * o + c, j, 0).start()
+                else:
+                    @pl.when(c != level)
+                    def _():
+                        part_copy(2 * o + c, j, 0).start()
+
+    kept = pltpu.make_async_copy(
+        partial.at[i, frame_rows(j, half), :], parts.at[0, level, place], r_recv
+    )
+    kept.start()
+
+    def add_up(sets):
+        for l in range(2):
+            sums = [jnp.sum(parts[s, l].astype(jnp.float32), axis=0) for s in range(sets)]
+            out[l] = sum(sums) / (count - 1)
+
+    @pl.when(outer)
+    def _():
+        pltpu.make_async_copy(parts.at[0], parts.at[0], r_recv).wait()
+        add_up(1)
+
+    @pl.when(jnp.logical_not(outer))
+    def _():
+        pltpu.make_async_copy(parts, parts, r_recv).wait()
+        add_up(2)
+
+    wait_blocks(3 * n_lon - 1, r_send)
+
+
+def member_plan(members, gradient, lon_taper, lat_taper):
+    n_lon, n_lat = lax.axis_size("lon"), lax.axis_size("lat")
+    count, levels, clat, clon = members.shape
+    share = count // n_lon
+    frame = 3 * clat
+    vmem = pl.BlockSpec(memory_space=pltpu.VMEM)
+    hbm = pl.BlockSpec(memory_space=pl.ANY)
+    dma = pltpu.SemaphoreType.DMA
+    return pl.pallas_call(
+        functools.partial(member_kernel, n_lon, n_lat, count),
+        out_shape=pltpu.VMEM(gradient.shape, jnp.float32),
+        in_specs=[hbm, hbm, hbm, hbm],
+        out_specs=vmem,
+        scratch_shapes=[
+            pltpu.VMEM(lon_taper.shape, lon_taper.dtype),
+            pltpu.VMEM(lat_taper.shape, lat_taper.dtype),
+            pltpu.VMEM((3, levels, clat, clon), jnp.float32),
+            pltpu.VMEM((n_lon, 3, clat, clon), jnp.float32),
+            pltpu.VMEM((share, n_lon, frame, clon), jnp.bfloat16),
+            pltpu.VMEM((n_lon // 2 * CHUNK * frame, 6 * clon), jnp.bfloat16),
+            pltpu.VMEM((n_lon // 2 * CHUNK * frame, 2 * clon), jnp.bfloat16),
+            pltpu.VMEM((n_lon // 2, frame, 2 * clon), jnp.float32),
+            pltpu.VMEM((6 * clon, 2 * clon), jnp.bfloat16),
+            pltpu.VMEM((frame, frame), jnp.bfloat16),
+            pltpu.VMEM((n_lon, frame, clon), jnp.bfloat16),
+            pltpu.VMEM((2, 2, n_lon, clat, clon), jnp.bfloat16),
+            dma((2,)), dma((3,)), dma((3,)), dma, dma((n_lon,)), dma((n_lon,)),
+            dma((share // CHUNK,)), dma((share // CHUNK,)), dma, dma,
+        ],
+        compiler_params=pltpu.CompilerParams(
+            collective_id=0, has_side_effects=True, vmem_limit_bytes=VMEM_BYTES
+        ),
+    )(members, gradient, lon_taper, lat_taper)
+
+
+def per_device(members, gradient, lon_taper, lat_taper):
+    n_lon, n_lat = lax.axis_size("lon"), lax.axis_size("lat")
+    count, levels, clat, clon = members.shape
+    cycle = levels == 2 and n_lon % 2 == 0 and n_lon >= 6
+    if cycle and n_lat == 4 and count % (n_lon * CHUNK) == 0 and count >= n_lon * n_lat * CHUNK:
+        return member_plan(members, gradient, lon_taper, lat_taper)
+    return halo_plan(members, gradient, lon_taper, lat_taper)
+
+
 def solution(mesh):
     in_specs = (P(None, None, "lat", "lon"), P(None, "lat", "lon"), P(), P())
     out_specs = P(None, "lat", "lon")

time: 620 us -> 44.3 us (0.07)
  local copies, waits for them, and re-layouts: 545 us -> 0.62 us
  waiting for transfers between devices: 48.2 us -> 0 us
  Pallas kernels: 0 us -> 43.5 us
  starting transfers between devices: 18.8 us -> 0 us
    gather x3 -> x0, local copies, waits for them, and re-layouts: 533 us -> none  [taper_table(): picked = jnp.take(weights, where_at, axis=0)]
    ppermute x8 -> x0, waiting for transfers between devices: 48.2 us -> none  [the longest x4 48.2 us: from_behind_2(): return lax.ppermute(block, axis, route)]
    pallas_call x0 -> x1, Pallas kernels: none -> 43.5 us  [member_plan(): pl.pallas_call(functools.partial(member_kernel, n_lon, n_lat, count), out...]
    ppermute x8 -> x0, starting transfers between devices: 18.8 us -> none  [the longest x4 13.1 us: from_behind_2(): return lax.ppermute(block, axis, route)]
    unnamed x15 -> x1, local copies, waits for them, and re-layouts: 10.3 us -> 0.62 us
  transfers between devices with their start and end apart: 8 -> 0, of which waited for: 2 -> 0; matrix products, arithmetic and copies ran while one was open for 88% -> 0% of each run, Pallas kernels for 0% -> 0%
where the time goes in v4:
time: 44.3 us; the launch traced here: 44.1 us
  Pallas kernels  43.5 us (98%)
  local copies, waits for them, and re-layouts  0.62 us (1%)
    pallas_call x1, Pallas kernels, member_plan(): pl.pallas_call(functools.partial(member_kernel, n_lon, n_lat, count), out...  43.5 us

profile of v4, /device:TPU:0, one launch (start us, length us, event | category | flops | bytes accessed | tf_op | source)
XLA Modules:
  0.0 44.1 jit_solution(8343470899979942140)
XLA Ops:
  0.0 43.5 %shard_map.46 = f32[2,32,128]{2,1,0:T(8,128)S(1)} custom-call(bf16[80,2,32,128]{3,2,1,0:T(8,128)(2,1)} %members.1, f32[2,32,128]{2,1,0:T(8,128)} %gradient.1, bf16[513]{0:T(1024)(128)(2,1)} %lon_taper.1, bf16[129]{0:T(256)(128)(2,1)} %lat_taper.1), custom_call_target="tpu_custom_call" | custom-call | tf_op jit(solution)/shard_map/pallas_call | solution.py:316
  43.5 0.6 %copy.6 = f32[2,32,128]{2,1,0:T(8,128)} copy(f32[2,32,128]{2,1,0:T(8,128)S(1)} %shard_map.46) | data formatting | bytes 65536

commit v5 on v4

--- a/solution.py
+++ b/solution.py
@@ -68,7 +68,7 @@
 def member_kernel(
     n_lon, n_lat, count,
     members, gradient, lon_taper, lat_taper, out,
-    lon_line, lat_line, grad_z, grad_all, taken, stack, along, total, lon_table, lat_table, partial, parts,
+    lon_line, lat_line, grad_z, grad_all, taken, stack, total, lon_table, lat_table, partial, parts,
     line_sem, gz_send, gz_recv, own_grad, ga_send, ga_recv, m_send, m_recv, r_send, r_recv,
 ):
     i, j = lax.axis_index("lon"), lax.axis_index("lat")
@@ -251,23 +251,26 @@
                     at = (b % 2 + 2 - 2 * step) * clon
                     row = o * span + e * frame
                     stack[row:row + frame, at:at + clon] = p
-        along_lon = jnp.dot(
-            stack[...], lon_table[...], preferred_element_type=jnp.float32
-        ).astype(jnp.bfloat16)
         if q < share // CHUNK - 1:
+            along_lon = jnp.dot(
+                stack[...], lon_table[...], preferred_element_type=jnp.float32
+            ).astype(jnp.bfloat16)
             for o in range(pairs):
                 for e in range(CHUNK):
                     row = o * span + e * frame
                     term = pair_term(q * CHUNK + e, o, along_lon[row:row + frame])
                     total[o] = term if q + e == 0 else total[o] + term
             continue
-        along[...] = along_lon
         for t in range(pairs):
             o = lax.rem(i // 2 + 1 + t, pairs)
+            window = stack[pl.ds(pl.multiple_of(o * span, span), span), :]
+            along_lon = jnp.dot(
+                window, lon_table[...], preferred_element_type=jnp.float32
+            ).astype(jnp.bfloat16)
             done = total[o]
             for e in range(CHUNK):
-                row = pl.multiple_of(o * span + e * frame, clat)
-                done += pair_term(q * CHUNK + e, o, along[pl.ds(row, frame), :])
+                row = e * frame
+                done += pair_term(q * CHUNK + e, o, along_lon[row:row + frame])
             for c in range(2):
                 partial[2 * o + c] = done[:, c * clon:(c + 1) * clon].astype(jnp.bfloat16)
             for c in range(2):
@@ -325,7 +328,6 @@
             pltpu.VMEM((n_lon, 3, clat, clon), jnp.float32),
             pltpu.VMEM((share, n_lon, frame, clon), jnp.bfloat16),
             pltpu.VMEM((n_lon // 2 * CHUNK * frame, 6 * clon), jnp.bfloat16),
-            pltpu.VMEM((n_lon // 2 * CHUNK * frame, 2 * clon), jnp.bfloat16),
             pltpu.VMEM((n_lon // 2, frame, 2 * clon), jnp.float32),
             pltpu.VMEM((6 * clon, 2 * clon), jnp.bfloat16),
             pltpu.VMEM((frame, frame), jnp.bfloat16),

time: 44.3 us -> 44.5 us (level)
  no operation moved by 1% of the time
where the time goes in v5:
time: 44.5 us; the launch traced here: 44.4 us
  Pallas kernels  43.7 us (98%)
  local copies, waits for them, and re-layouts  0.62 us (1%)
    pallas_call x1, Pallas kernels, member_plan(): pl.pallas_call(functools.partial(member_kernel, n_lon, n_lat, count), out...  43.7 us

profile of v5, /device:TPU:0, one launch (start us, length us, event | category | flops | bytes accessed | tf_op | source)
XLA Modules:
  0.0 44.4 jit_solution(14429690957964220347)
XLA Ops:
  0.0 43.7 %shard_map.46 = f32[2,32,128]{2,1,0:T(8,128)S(1)} custom-call(bf16[80,2,32,128]{3,2,1,0:T(8,128)(2,1)} %members.1, f32[2,32,128]{2,1,0:T(8,128)} %gradient.1, bf16[513]{0:T(1024)(128)(2,1)} %lon_taper.1, bf16[129]{0:T(256)(128)(2,1)} %lat_taper.1), custom_call_target="tpu_custom_call" | custom-call | tf_op jit(solution)/shard_map/pallas_call | solution.py:319
  43.8 0.6 %copy.6 = f32[2,32,128]{2,1,0:T(8,128)} copy(f32[2,32,128]{2,1,0:T(8,128)S(1)} %shard_map.46) | data formatting | bytes 65536

commit v6 on v4

--- a/solution.py
+++ b/solution.py
@@ -92,19 +92,95 @@
     def frame_rows(j_at, in_half):
         return pl.ds(pl.multiple_of((j_at - in_half) * clat, clat), clat)
 
+    barrier = pltpu.get_barrier_semaphore()
+
+    def greet(k, c):
+        i_to, j_to = other(k)
+
+        @pl.when((j_to - j != n_lat - 1) & (j - j_to != n_lat - 1))
+        def _():
+            pl.semaphore_signal(barrier, inc=1, device_id={"lon": i_to, "lat": j_to}, device_id_type=MESH)
+
+        return c
+
+    lax.fori_loop(1, n, greet, 0)
+
+    @pl.when(outer)
+    def _():
+        pl.semaphore_wait(barrier, n - n_lon - 1)
+
+    @pl.when(jnp.logical_not(outer))
+    def _():
+        pl.semaphore_wait(barrier, n - 1)
+
+
+    def grad_z_copy(j_to, slot):
+        return pltpu.make_async_remote_copy(
+            src_ref=gradient, dst_ref=grad_z.at[j - j_to // 2],
+            send_sem=gz_send.at[slot], recv_sem=gz_recv.at[j - j_to // 2],
+            device_id={"lon": i, "lat": j_to}, device_id_type=MESH,
+        )
+
+    across = 2 - 2 * half
+
+    def start_members(q):
+        def to_half(first):
+            def start(k, c):
+                i_to = lax.rem(i + lax.rem(k, n_lon), n_lon)
+                j_to = first + lax.rem(j + k // n_lon, 2)
+                at = ((i_to // 2) * 2 + lax.rem(j_to, 2)) * share + q * CHUNK
+
+                @pl.when((i_to != i) | (j_to != j))
+                def _():
+                    pltpu.make_async_remote_copy(
+                        src_ref=members.at[pl.ds(at, CHUNK), lax.rem(i_to, 2)],
+                        dst_ref=taken.at[pl.ds(q * CHUNK, CHUNK), i, frame_rows(j, first // 2), :],
+                        send_sem=m_send.at[q], recv_sem=m_recv.at[q],
+                        device_id={"lon": i_to, "lat": j_to}, device_id_type=MESH,
+                    ).start()
+
+                return c
+
+            lax.fori_loop(0, 2 * n_lon, start, 0)
+
+        @pl.when(jnp.logical_not(outer))
+        def _():
+            to_half(across)
+
+        to_half(2 * half)
+
+    def wait_blocks(count, sem):
+        sent = members.at[pl.ds(0, count), 0]
+        pltpu.make_async_copy(sent, sent, sem).wait()
+
+    def wait_members(q):
+        here = taken.at[pl.ds(q * CHUNK, CHUNK)]
+        pltpu.make_async_copy(here, here, m_recv.at[q]).wait()
+        wait_blocks((n // 2 - 1) * CHUNK, m_send.at[q])
+
+        @pl.when(jnp.logical_not(outer))
+        def _():
+            wait_blocks(n // 2 * CHUNK, m_send.at[q])
+
+    def grad_all_copy(k):
+        i_to = lax.rem(i + k, n_lon)
+        return pltpu.make_async_remote_copy(
+            src_ref=grad_z.at[:, lax.rem(i_to, 2)], dst_ref=grad_all.at[i],
+            send_sem=ga_send.at[i_to], recv_sem=ga_recv.at[i],
+            device_id={"lon": i_to, "lat": j}, device_id_type=MESH,
+        )
+
+    @pl.when(jnp.logical_not(outer))
+    def _():
+        for c in range(2):
+            grad_z_copy(across + c, 1 + c).start()
+
+    grad_z_copy(mate, 0).start()
+    start_members(0)
     lon_in = pltpu.make_async_copy(lon_taper, lon_line, line_sem.at[0])
     lat_in = pltpu.make_async_copy(lat_taper, lat_line, line_sem.at[1])
     lon_in.start()
     lat_in.start()
-
-    barrier = pltpu.get_barrier_semaphore()
-
-    def greet(k, c):
-        i_to, j_to = other(k)
-        pl.semaphore_signal(barrier, inc=1, device_id={"lon": i_to, "lat": j_to}, device_id_type=MESH)
-        return c
-
-    lax.fori_loop(1, n, greet, 0)
 
     own = pltpu.make_async_copy(gradient, grad_z.at[j - half], own_grad)
     own.start()
@@ -114,6 +190,24 @@
             taken.at[pl.ds(q * CHUNK, CHUNK), i, frame_rows(j, half), :], m_recv.at[q],
         ).start()
 
+    own.wait()
+    grad_z_copy(mate, 0).wait_send()
+
+    @pl.when(jnp.logical_not(outer))
+    def _():
+        for c in range(2):
+            grad_z_copy(across + c, 1 + c).wait_send()
+
+    for j_from in (mate, beside):
+        pltpu.make_async_remote_copy(
+            src_ref=gradient, dst_ref=grad_z.at[j_from - half],
+            send_sem=gz_send.at[0], recv_sem=gz_recv.at[j_from - half],
+            device_id={"lon": i, "lat": j_from}, device_id_type=MESH,
+        ).wait_recv()
+    for k in range(1, n_lon):
+        grad_all_copy(k).start()
+    for q in range(1, share // CHUNK):
+        start_members(q)
     def centred(values, length):
         values = values.astype(jnp.float32).reshape(1, values.shape[0])
         side = (length - values.shape[1] + 1) // 2
@@ -135,89 +229,6 @@
     kept_here = (to_block != 2 - 2 * half) | (from_block == 2 * half)
     lat_table[...] = jnp.where(kept_here, whole, 0.0).astype(jnp.bfloat16)
 
-    pl.semaphore_wait(barrier, n - 1)
-    own.wait()
-
-    def grad_z_copy(j_to, slot):
-        return pltpu.make_async_remote_copy(
-            src_ref=gradient, dst_ref=grad_z.at[j - j_to // 2],
-            send_sem=gz_send.at[slot], recv_sem=gz_recv.at[j - j_to // 2],
-            device_id={"lon": i, "lat": j_to}, device_id_type=MESH,
-        )
-
-    across = 2 - 2 * half
-
-    def start_members(q):
-        def to_half(first):
-            def start(k, c):
-                i_to = lax.rem(i + lax.rem(k, n_lon), n_lon)
-                j_to = first + lax.rem(j + k // n_lon, 2)
-                at = ((i_to // 2) * 2 + lax.rem(j_to, 2)) * share + q * CHUNK
-
-                @pl.when((i_to != i) | (j_to != j))
-                def _():
-                    pltpu.make_async_remote_copy(
-                        src_ref=members.at[pl.ds(at, CHUNK), lax.rem(i_to, 2)],
-                        dst_ref=taken.at[pl.ds(q * CHUNK, CHUNK), i, frame_rows(j, first // 2), :],
-                        send_sem=m_send.at[q], recv_sem=m_recv.at[q],
-                        device_id={"lon": i_to, "lat": j_to}, device_id_type=MESH,
-                    ).start()
-
-                return c
-
-            lax.fori_loop(0, 2 * n_lon, start, 0)
-
-        @pl.when(jnp.logical_not(outer))
-        def _():
-            to_half(across)
-
-        to_half(2 * half)
-
-    def wait_blocks(count, sem):
-        sent = members.at[pl.ds(0, count), 0]
-        pltpu.make_async_copy(sent, sent, sem).wait()
-
-    def wait_members(q):
-        here = taken.at[pl.ds(q * CHUNK, CHUNK)]
-        pltpu.make_async_copy(here, here, m_recv.at[q]).wait()
-        wait_blocks((n // 2 - 1) * CHUNK, m_send.at[q])
-
-        @pl.when(jnp.logical_not(outer))
-        def _():
-            wait_blocks(n // 2 * CHUNK, m_send.at[q])
-
-    def grad_all_copy(k):
-        i_to = lax.rem(i + k, n_lon)
-        return pltpu.make_async_remote_copy(
-            src_ref=grad_z.at[:, lax.rem(i_to, 2)], dst_ref=grad_all.at[i],
-            send_sem=ga_send.at[i_to], recv_sem=ga_recv.at[i],
-            device_id={"lon": i_to, "lat": j}, device_id_type=MESH,
-        )
-
-    @pl.when(jnp.logical_not(outer))
-    def _():
-        for c in range(2):
-            grad_z_copy(across + c, 1 + c).start()
-
-    grad_z_copy(mate, 0).start()
-    start_members(0)
-    grad_z_copy(mate, 0).wait_send()
-
-    @pl.when(jnp.logical_not(outer))
-    def _():
-        for c in range(2):
-            grad_z_copy(across + c, 1 + c).wait_send()
-
-    for j_from in (mate, beside):
-        pltpu.make_async_remote_copy(
-            src_ref=gradient, dst_ref=grad_z.at[j_from - half],
-            send_sem=gz_send.at[0], recv_sem=gz_recv.at[j_from - half],
-            device_id={"lon": i, "lat": j_from}, device_id_type=MESH,
-        ).wait_recv()
-    for k in range(1, n_lon):
-        grad_all_copy(k).start()
-    for q in range(1, share // CHUNK):
-        start_members(q)
     grad_all[i] = grad_z[:, level]
     for k in range(1, n_lon):
         i_from = lax.rem(i + k, n_lon)

time: 44.3 us -> 44.3 us (level)
  no operation moved by 1% of the time
where the time goes in v6:
time: 44.3 us; the launch traced here: 44.1 us
  Pallas kernels  43.4 us (98%)
  local copies, waits for them, and re-layouts  0.62 us (1%)
    pallas_call x1, Pallas kernels, member_plan(): pl.pallas_call(functools.partial(member_kernel, n_lon, n_lat, count), out...  43.4 us

profile of v6, /device:TPU:0, one launch (start us, length us, event | category | flops | bytes accessed | tf_op | source)
XLA Modules:
  0.0 44.1 jit_solution(10759017548780874116)
XLA Ops:
  0.0 43.4 %shard_map.46 = f32[2,32,128]{2,1,0:T(8,128)S(1)} custom-call(bf16[80,2,32,128]{3,2,1,0:T(8,128)(2,1)} %members.1, f32[2,32,128]{2,1,0:T(8,128)} %gradient.1, bf16[513]{0:T(1024)(128)(2,1)} %lon_taper.1, bf16[129]{0:T(256)(128)(2,1)} %lat_taper.1), custom_call_target="tpu_custom_call" | custom-call | tf_op jit(solution)/shard_map/pallas_call | solution.py:327
  43.5 0.6 %copy.6 = f32[2,32,128]{2,1,0:T(8,128)} copy(f32[2,32,128]{2,1,0:T(8,128)S(1)} %shard_map.46) | data formatting | bytes 65536
